TPU v7x, 128 devices: a whole 4x4x4 slice. The times are simulated.
128 devices in a mesh: rep: 16 (over y, z_hi, core), shard: 8 (over z_lo, x).
Axes of the slice: x: 4, y: 4, z: 4 (z_hi: 2, z_lo: 2; z = z_hi * 2 + z_lo), core: 2. Of those that a mesh axis runs over, the one named last changes fastest.
Arguments:
- tokens: bfloat16 [16384, 2048], P(('rep', 'shard')), may hold values from -6 to 6
- doc_lengths: int32 [128, 3], P(('rep', 'shard')), may hold values from 1 to 64, 128 in all within a row
- cotangent: bfloat16 [16384, 2048], P(('rep', 'shard')), may hold values from -6 to 6
- ln1_gain: bfloat16 [2048], P('shard'), may hold values from 0.5 to 1.5
- ln1_bias: bfloat16 [2048], P('shard'), may hold values from -1.5 to 1.5
- ln2_gain: bfloat16 [2048], P('shard'), may hold values from 0.5 to 1.5
- ln2_bias: bfloat16 [2048], P('shard'), may hold values from -1.5 to 1.5
- qkv_weight: bfloat16 [2048, 6144], P('shard'), may hold values from -0.125 to 0.125
- qkv_bias: bfloat16 [6144], P('shard'), may hold values from -3 to 3
- out_weight: bfloat16 [2048, 2048], P('shard'), may hold values from -0.5 to 0.5
- out_bias: bfloat16 [2048], P('shard'), may hold values from -3 to 3
- up_weight: bfloat16 [2048, 8192], P('shard'), may hold values from -0.125 to 0.125
- up_bias: bfloat16 [8192], P('shard'), may hold values from -3 to 3
- down_weight: bfloat16 [8192, 2048], P('shard'), may hold values from -0.09375 to 0.09375
- down_bias: bfloat16 [2048], P('shard'), may hold values from -3 to 3
Outputs:
- mixed: bfloat16 [16384, 2048], P(('rep', 'shard'))
- tokens_grad: float32 [16384, 2048], P(('rep', 'shard'))
- ln1_gain_grad: float32 [2048], P('shard')
- ln1_bias_grad: float32 [2048], P('shard')
- ln2_gain_grad: float32 [2048], P('shard')
- ln2_bias_grad: float32 [2048], P('shard')
- qkv_weight_grad: float32 [2048, 6144], P('shard')
- qkv_bias_grad: float32 [6144], P('shard')
- out_weight_grad: float32 [2048, 2048], P('shard')
- out_bias_grad: float32 [2048], P('shard')
- up_weight_grad: float32 [2048, 8192], P('shard')
- up_bias_grad: float32 [8192], P('shard')
- down_weight_grad: float32 [8192, 2048], P('shard')
- down_bias_grad: float32 [2048], P('shard')
Inputs may be any that keep to these rules, and one draw needn't show every extreme that they name: `doc_lengths`: each row sums to 128; some document has exactly 64 tokens.
All inputs are finite; a program needn't handle non-finite values.
Results may differ from a plain program's by a relative error of at most 0.02.
Values may be sent and summed in bfloat16 or wider, within the bound.
No kernel may reach another device: no remote copies, remote signals or barrier semaphores. Data moves between devices by JAX's collectives and lax.ppermute only.
A program may use at most 448 MiB of HBM per device.

v0:
```python
import math

import jax
import jax.numpy as jnp
from jax import lax
from jax.sharding import PartitionSpec as P

HEADS = 8
ROT = 64


EPS = 1e-05


def norm_parts(value, gain, bias):
    centre = value - jnp.mean(value, -1, keepdims=True)
    inverse = lax.rsqrt(jnp.mean(centre * centre, -1, keepdims=True) + EPS)
    normed = centre * inverse
    return (normed * gain + bias, normed, inverse)


def norm_back(grad, normed, inverse, gain):
    gain_grad = jnp.sum(grad * normed, 0)
    bias_grad = jnp.sum(grad, 0)
    scaled = grad * gain
    back = inverse * (
        scaled
        - jnp.mean(scaled, -1, keepdims=True)
        - normed * jnp.mean(scaled * normed, -1, keepdims=True)
    )
    return (back, gain_grad, bias_grad)


def rotate(value, cosine, sine):
    half = ROT // 2
    first = value[..., :half]
    second = value[..., half:ROT]
    return jnp.concatenate(
        [first * cosine - second * sine, second * cosine + first * sine, value[..., ROT:]], -1
    )


def unrotate(grad, cosine, sine):
    half = ROT // 2
    first = grad[..., :half]
    second = grad[..., half:ROT]
    return jnp.concatenate(
        [first * cosine + second * sine, second * cosine - first * sine, grad[..., ROT:]], -1
    )


def gelu_slope(hidden):
    normal_cdf = 0.5 * (1.0 + jax.scipy.special.erf(hidden / math.sqrt(2.0)))
    normal_pdf = jnp.exp(-0.5 * hidden * hidden) / math.sqrt(2.0 * math.pi)
    return normal_cdf + hidden * normal_pdf


def local(
    tokens,
    doc_lengths,
    cotangent,
    ln1_gain,
    ln1_bias,
    ln2_gain,
    ln2_bias,
    qkv_weight,
    qkv_bias,
    out_weight,
    out_bias,
    up_weight,
    up_bias,
    down_weight,
    down_bias,
):
    f32 = jnp.float32
    bf16 = jnp.bfloat16
    g1, b1, g2, b2, w_qkv, b_qkv, w_out, b_out, w_up, b_up, w_down, b_down = (
        lax.all_gather(ln1_gain, "shard", axis=0, tiled=True),
        lax.all_gather(ln1_bias, "shard", axis=0, tiled=True),
        lax.all_gather(ln2_gain, "shard", axis=0, tiled=True),
        lax.all_gather(ln2_bias, "shard", axis=0, tiled=True),
        lax.all_gather(qkv_weight, "shard", axis=0, tiled=True),
        lax.all_gather(qkv_bias, "shard", axis=0, tiled=True),
        lax.all_gather(out_weight, "shard", axis=0, tiled=True),
        lax.all_gather(out_bias, "shard", axis=0, tiled=True),
        lax.all_gather(up_weight, "shard", axis=0, tiled=True),
        lax.all_gather(up_bias, "shard", axis=0, tiled=True),
        lax.all_gather(down_weight, "shard", axis=0, tiled=True),
        lax.all_gather(down_bias, "shard", axis=0, tiled=True),
    )
    rows = tokens.shape[0]
    width = tokens.shape[1]
    head_size = width // HEADS
    scale = head_size ** (-0.5)
    lengths = doc_lengths[0]
    ends = jnp.cumsum(lengths)
    starts = ends - lengths
    steps_t = jnp.arange(rows, dtype=jnp.int32)
    segment = jnp.sum((steps_t[:, None] >= ends[None, :]).astype(jnp.int32), 1)
    slots = jnp.arange(lengths.shape[0], dtype=jnp.int32)
    begin = jnp.sum(jnp.where(segment[:, None] == slots[None, :], starts[None, :], 0), 1)
    position = (steps_t - begin).astype(f32)
    freq = 10000.0 ** (-2.0 * jnp.arange(ROT // 2, dtype=f32) / ROT)
    angle = position[:, None, None] * freq[None, None, :]
    cosine = jnp.cos(angle)
    sine = jnp.sin(angle)
    allowed = (segment[:, None] == segment[None, :]) & (steps_t[None, :] <= steps_t[:, None])
    xf = tokens.astype(f32)
    n1, normed1, inverse1 = norm_parts(xf, g1.astype(f32), b1.astype(f32))
    n2, normed2, inverse2 = norm_parts(xf, g2.astype(f32), b2.astype(f32))
    h1 = n1.astype(bf16)
    h2 = n2.astype(bf16)
    qkv = jnp.dot(h1, w_qkv, preferred_element_type=f32) + b_qkv.astype(f32)
    query = qkv[:, :width].reshape(rows, HEADS, head_size)
    key = qkv[:, width : 2 * width].reshape(rows, HEADS, head_size)
    ql = rotate(query, cosine, sine).astype(bf16)
    kl = rotate(key, cosine, sine).astype(bf16)
    vl = qkv[:, 2 * width :].reshape(rows, HEADS, head_size).astype(bf16)
    scores = jnp.einsum("qhd,khd->hqk", ql, kl, preferred_element_type=f32) * scale
    masked = jnp.where(allowed[None], scores, -1e30)
    shifted = jnp.exp(masked - jnp.max(masked, -1, keepdims=True))
    probs = shifted / jnp.sum(shifted, -1, keepdims=True)
    probs_low = probs.astype(bf16)
    attended = (
        jnp.einsum("hqk,khd->qhd", probs_low, vl, preferred_element_type=f32)
        .reshape(rows, width)
        .astype(bf16)
    )
    branch_attn = jnp.dot(attended, w_out, preferred_element_type=f32) + b_out.astype(f32)
    hidden = jnp.dot(h2, w_up, preferred_element_type=f32) + b_up.astype(f32)
    active = jax.nn.gelu(hidden, approximate=False).astype(bf16)
    branch_ff = jnp.dot(active, w_down, preferred_element_type=f32) + b_down.astype(f32)
    mixed = (xf + branch_attn + branch_ff).astype(bf16)
    dyf = cotangent.astype(f32)
    d_down_w = jnp.dot(active.T, cotangent, preferred_element_type=f32)
    d_out_w = jnp.dot(attended.T, cotangent, preferred_element_type=f32)
    d_dy_b = jnp.sum(dyf, 0)
    s_down_w, s_down_b = (
        lax.psum_scatter(
            d_down_w.astype(jnp.bfloat16), "shard", scatter_dimension=0, tiled=True
        ).astype(jnp.float32),
        lax.psum_scatter(
            d_dy_b.astype(jnp.bfloat16), "shard", scatter_dimension=0, tiled=True
        ).astype(jnp.float32),
    )
    s_out_w, s_out_b = (
        lax.psum_scatter(
            d_out_w.astype(jnp.bfloat16), "shard", scatter_dimension=0, tiled=True
        ).astype(jnp.float32),
        lax.psum_scatter(
            d_dy_b.astype(jnp.bfloat16), "shard", scatter_dimension=0, tiled=True
        ).astype(jnp.float32),
    )
    d_active = jnp.dot(cotangent, w_down.T, preferred_element_type=f32)
    d_hidden = (d_active * gelu_slope(hidden)).astype(bf16)
    d_h2 = jnp.dot(d_hidden, w_up.T, preferred_element_type=f32)
    d_up_w = jnp.dot(h2.T, d_hidden, preferred_element_type=f32)
    d_up_b = jnp.sum(d_hidden.astype(f32), 0)
    s_up_w, s_up_b = (
        lax.psum_scatter(
            d_up_w.astype(jnp.bfloat16), "shard", scatter_dimension=0, tiled=True
        ).astype(jnp.float32),
        lax.psum_scatter(
            d_up_b.astype(jnp.bfloat16), "shard", scatter_dimension=0, tiled=True
        ).astype(jnp.float32),
    )
    d_attended = (
        jnp.dot(cotangent, w_out.T, preferred_element_type=f32)
        .astype(bf16)
        .reshape(rows, HEADS, head_size)
    )
    d_value = jnp.einsum("hqk,qhd->khd", probs_low, d_attended, preferred_element_type=f32)
    d_probs = jnp.einsum("qhd,khd->hqk", d_attended, vl, preferred_element_type=f32)
    centred = d_probs - jnp.sum(d_probs * probs, -1, keepdims=True)
    d_scores = (probs * centred).astype(bf16)
    d_query = jnp.einsum("hqk,khd->qhd", d_scores, kl, preferred_element_type=f32) * scale
    d_key = jnp.einsum("hqk,qhd->khd", d_scores, ql, preferred_element_type=f32) * scale
    d_query = unrotate(d_query, cosine, sine)
    d_key = unrotate(d_key, cosine, sine)
    d_qkv = jnp.concatenate(
        [d_query.reshape(rows, width), d_key.reshape(rows, width), d_value.reshape(rows, width)], 1
    ).astype(bf16)
    d_h1 = jnp.dot(d_qkv, w_qkv.T, preferred_element_type=f32)
    back1, d_g1, d_b1 = norm_back(d_h1, normed1, inverse1, g1.astype(f32))
    back2, d_g2, d_b2 = norm_back(d_h2, normed2, inverse2, g2.astype(f32))
    tokens_grad = dyf + back1 + back2
    d_qkv_w = jnp.dot(h1.T, d_qkv, preferred_element_type=f32)
    d_qkv_b = jnp.sum(d_qkv.astype(f32), 0)
    s_qkv_w, s_qkv_b, s_g1, s_b1, s_g2, s_b2 = (
        lax.psum_scatter(
            d_qkv_w.astype(jnp.bfloat16), "shard", scatter_dimension=0, tiled=True
        ).astype(jnp.float32),
        lax.psum_scatter(
            d_qkv_b.astype(jnp.bfloat16), "shard", scatter_dimension=0, tiled=True
        ).astype(jnp.float32),
        lax.psum_scatter(
            d_g1.astype(jnp.bfloat16), "shard", scatter_dimension=0, tiled=True
        ).astype(jnp.float32),
        lax.psum_scatter(
            d_b1.astype(jnp.bfloat16), "shard", scatter_dimension=0, tiled=True
        ).astype(jnp.float32),
        lax.psum_scatter(
            d_g2.astype(jnp.bfloat16), "shard", scatter_dimension=0, tiled=True
        ).astype(jnp.float32),
        lax.psum_scatter(
            d_b2.astype(jnp.bfloat16), "shard", scatter_dimension=0, tiled=True
        ).astype(jnp.float32),
    )
    totals = (
        lax.psum(s_g1.astype(jnp.bfloat16), "rep").astype(jnp.float32),
        lax.psum(s_b1.astype(jnp.bfloat16), "rep").astype(jnp.float32),
        lax.psum(s_g2.astype(jnp.bfloat16), "rep").astype(jnp.float32),
        lax.psum(s_b2.astype(jnp.bfloat16), "rep").astype(jnp.float32),
        lax.psum(s_qkv_w.astype(jnp.bfloat16), "rep").astype(jnp.float32),
        lax.psum(s_qkv_b.astype(jnp.bfloat16), "rep").astype(jnp.float32),
        lax.psum(s_out_w.astype(jnp.bfloat16), "rep").astype(jnp.float32),
        lax.psum(s_out_b.astype(jnp.bfloat16), "rep").astype(jnp.float32),
        lax.psum(s_up_w.astype(jnp.bfloat16), "rep").astype(jnp.float32),
        lax.psum(s_up_b.astype(jnp.bfloat16), "rep").astype(jnp.float32),
        lax.psum(s_down_w.astype(jnp.bfloat16), "rep").astype(jnp.float32),
        lax.psum(s_down_b.astype(jnp.bfloat16), "rep").astype(jnp.float32),
    )
    return (
        mixed,
        tokens_grad,
        totals[0],
        totals[1],
        totals[2],
        totals[3],
        totals[4],
        totals[5],
        totals[6],
        totals[7],
        totals[8],
        totals[9],
        totals[10],
        totals[11],
    )


def solution(mesh):
    return jax.shard_map(
        local,
        mesh=mesh,
        in_specs=(
            P(("rep", "shard"), None),
            P(("rep", "shard"), None),
            P(("rep", "shard"), None),
            P("shard"),
            P("shard"),
            P("shard"),
            P("shard"),
            P("shard", None),
            P("shard"),
            P("shard", None),
            P("shard"),
            P("shard", None),
            P("shard"),
            P("shard", None),
            P("shard"),
        ),
        out_specs=(
            P(("rep", "shard"), None),
            P(("rep", "shard"), None),
            P("shard"),
            P("shard"),
            P("shard"),
            P("shard"),
            P("shard", None),
            P("shard"),
            P("shard", None),
            P("shard"),
            P("shard", None),
            P("shard"),
            P("shard", None),
            P("shard"),
        ),
        check_vma=False,
    )
```

profile of v0, /device:TPU:1, one launch (start us, length us, event | category | flops | bytes accessed | tf_op | source)
XLA Modules:
  0.0 2328.5 jit_solution(7242319322347223128)
XLA Ops:
  10.1 16.7 all-gather.1
  26.8 13.2 all-gather
  40.1 24.3 %all-gather.2 = bf16[8,1,768]{2,1,0:T(2,128)(2,1)S(1)} all-gather(bf16[1,1,768]{2,1,0:T(2,128)(2,1)S(1)} %reshape.224), channel_id=1, replica_groups=mesh['rep'=16,'shard'=8] {'shard'}, dimensions={0}, use_global_device_ids=true | all-gather | bytes 13824 | tf_op jit(solution)/shard_map/all_gather | solution.py:83
  65.7 196.9 %all-gather.12.cloned.1.call-done = bf16[2048,6144]{1,0:T(8,128)(2,1)} async-done(((bf16[256,6144]{1,0:T(8,128)(2,1)}), bf16[2048,6144]{1,0:T(8,128)(2,1)}) %all-gather.12.cloned.1.call-update) | async-done | bytes 25165840 | tf_op jit(solution)/shard_map/all_gather | solution.py:82
  262.5 10.1 convolution_add_fusion.1
  280.6 5.7 convolution_convert_fusion.3
  286.7 68.0 %all-gather.14.cloned.1.call-done = bf16[2048,2048]{1,0:T(8,128)(2,1)} async-done(((bf16[256,2048]{1,0:T(8,128)(2,1)}), bf16[2048,2048]{1,0:T(8,128)(2,1)}) %all-gather.14.cloned.1.call-update) | async-done | bytes 8388624 | tf_op jit(solution)/shard_map/all_gather | solution.py:84
  354.7 6.3 convolution_convert_fusion.4
  373.4 14.9 convolution_convert_fusion.2
  389.0 13.9 all-gather.5
  403.0 14.0 all-gather.4
  417.0 21.6 all_gather.45
  438.6 244.9 %all-gather.16.cloned.1.call-done = bf16[2048,8192]{1,0:T(8,128)(2,1)} async-done(((bf16[256,8192]{1,0:T(8,128)(2,1)}), bf16[2048,8192]{1,0:T(8,128)(2,1)}) %all-gather.16.cloned.1.call-update) | async-done | bytes 33554448 | tf_op jit(solution)/shard_map/all_gather | solution.py:86
  683.5 13.5 convolution_add_fusion
  699.0 20.7 convolution_convert_fusion.1
  720.0 291.4 %all-gather.18.cloned.1.call-done = bf16[8192,2048]{1,0:T(8,128)(2,1)} async-done(((bf16[1024,2048]{1,0:T(8,128)(2,1)}), bf16[8192,2048]{1,0:T(8,128)(2,1)}) %all-gather.18.cloned.1.call-update) | async-done | bytes 33554448 | tf_op jit(solution)/shard_map/all_gather | solution.py:88
  1011.4 17.9 fusion.70
  1029.3 14.0 convolution_convert_fusion
  1043.4 62.4 %reduce-scatter.7.cloned.1.call-done = bf16[256,2048]{1,0:T(8,128)(2,1)} async-done(((bf16[2048,2048]{1,0:T(8,128)(2,1)}), bf16[256,2048]{1,0:T(8,128)(2,1)}) %reduce-scatter.7.cloned.1.call-update) | async-done | bytes 1048592 | tf_op jit(solution)/shard_map/reduce_scatter | solution.py:147
  1105.8 251.4 %reduce-scatter.5.cloned.1.call-done = bf16[256,6144]{1,0:T(8,128)(2,1)} async-done(((bf16[2048,6144]{1,0:T(8,128)(2,1)}), bf16[256,6144]{1,0:T(8,128)(2,1)}) %reduce-scatter.5.cloned.1.call-update) | async-done | bytes 3145744 | tf_op jit(solution)/shard_map/reduce_scatter | solution.py:190
  1357.2 329.9 %reduce-scatter.11.cloned.1.call-done = bf16[1024,2048]{1,0:T(8,128)(2,1)} async-done(((bf16[8192,2048]{1,0:T(8,128)(2,1)}), bf16[1024,2048]{1,0:T(8,128)(2,1)}) %reduce-scatter.11.cloned.1.call-update) | async-done | bytes 4194320 | tf_op jit(solution)/shard_map/reduce_scatter | solution.py:139
  1687.1 330.0 %reduce-scatter.9.cloned.1.call-done = bf16[256,8192]{1,0:T(8,128)(2,1)} async-done(((bf16[2048,8192]{1,0:T(8,128)(2,1)}), bf16[256,8192]{1,0:T(8,128)(2,1)}) %reduce-scatter.9.cloned.1.call-update) | async-done | bytes 4194320 | tf_op jit(solution)/shard_map/reduce_scatter | solution.py:160
  2020.4 12.2 all-gather.6
  2032.7 14.1 all-gather.3
  2048.6 6.0 fusion.17
  2054.6 17.0 fusion.71
  2071.6 14.4 fusion.46
  2086.0 26.8 %all-reduce.9 = (bf16[2048]{0:T(1024)(128)(2,1)S(1)}, bf16[2048]{0:T(1024)(128)(2,1)S(1)}, bf16[2048]{0:T(1024)(128)(2,1)S(1)}, bf16[2048]{0:T(1024)(128)(2,1)S(...) all-reduce(bf16[2048]{0:T(1024)(128)(2,1)S(1)} %get-tuple-element.1, ...), channel_id=2, replica_groups=mesh['rep'=16,'shard'=8] {'shard'}, use_global_device_ids=true, to_apply=%region_13.14.clone | all-reduce | flops 24576 | bytes 98304
  2113.2 46.8 %all-reduce.7 = (bf16[256]{0:T(256)(128)(2,1)S(1)}, bf16[256]{0:T(256)(128)(2,1)S(1)}, bf16[256]{0:T(256)(128)(2,1)S(1)}, bf16[256]{0:T(256)(128)(2,1)S(1)}, bf1...) all-reduce(bf16[256]{0:T(256)(128)(2,1)S(1)} %dynamic-slice.1, ...), channel_id=1, replica_groups=mesh['rep'=16,'shard'=8] {'rep'}, use_global_device_ids=true, to_apply=%region_14.15 | all-reduce | flops 3072 | bytes 12288 | tf_op jit(solution)/shard_map/psum | solution.py:210
  2165.2 18.4 fusion.18
  2183.6 122.4 %all-reduce.12.cloned.1.call-done = (bf16[256,6144]{1,0:T(8,128)(2,1)}, bf16[256,2048]{1,0:T(8,128)(2,1)}, bf16[256,8192]{1,0:T(8,128)(2,1)}, bf16[1024,2048]{1,0:T(8,128)(2,1)}) async-done(((bf16[256,6144]{1,0:T(8,128)(2,1)}, bf16[256,2048]{1,0:T(8,128)(2,1)}, bf16[256,8192]{1,0:T(8,128)(2,1)}, bf16[1024,2048]{1,0:T(8,128)(2,1)}), (bf16[256,6144]{1,0:T(8,128)(2,1)}, bf16[256,2048]{1,0:T(8,128)(2,1)}, ...) | async-done | bytes 12582928 | tf_op jit(solution)/shard_map/psum | solution.py:214
  2316.8 4.4 convert_element_type.212
  (166 shorter events, 47.6 us)
Async XLA Ops:
  7.2 255.3 %all-gather.12.cloned.1.call-start = ((), (), s32[]{:S(2)}) async-start(), calls=%async_computation.4 | async-start | bytes 28311552 | tf_op jit(solution)/shard_map/all_gather | solution.py:82
  7.9 346.8 %all-gather.14.cloned.1.call-start = ((), (), s32[]{:S(2)}) async-start(), calls=%async_computation.5 | async-start | bytes 9437184 | tf_op jit(solution)/shard_map/all_gather | solution.py:84
  8.7 55.7 %copy-start.29 = (s32[1,3]{1,0:T(1,128)S(1)}, s32[1,3]{1,0:T(1,128)}, u32[]{:S(2)}) copy-start(s32[1,3]{1,0:T(1,128)} %param.16) | copy-start | bytes 40
  8.7 56.0 %copy-start = (bf16[128,2048]{1,0:T(8,128)(2,1)S(1)}, bf16[128,2048]{1,0:T(8,128)(2,1)}, u32[]{:S(2)}) copy-start(bf16[128,2048]{1,0:T(8,128)(2,1)} %param.15) | copy-start | bytes 1572868
  8.7 674.8 %all-gather.16.cloned.1.call-start = ((), (), s32[]{:S(2)}) async-start(), calls=%async_computation.6 | async-start | bytes 37748736 | tf_op jit(solution)/shard_map/all_gather | solution.py:86
  9.4 1002.0 %all-gather.18.cloned.1.call-start = ((), (), s32[]{:S(2)}) async-start(), calls=%async_computation.7 | async-start | bytes 37748736 | tf_op jit(solution)/shard_map/all_gather | solution.py:88
  10.0 1095.8 %reduce-scatter.7.cloned.1.call-start = ((), (), s32[]{:S(2)}) async-start(), calls=%async_computation.9 | async-start | bytes 9437184 | tf_op jit(solution)/shard_map/reduce_scatter | solution.py:147
  64.9 207.7 %copy-start.18 = (f32[128]{0:T(128)}, f32[128]{0:T(128)S(1)}, u32[]{:S(2)}) copy-start(f32[128]{0:T(128)S(1)} %broadcast_multiply_fusion.4) | copy-start | bytes 1540
  65.2 207.4 %copy-start.20 = (f32[128]{0:T(128)}, f32[128]{0:T(128)S(1)}, u32[]{:S(2)}) copy-start(f32[128]{0:T(128)S(1)} %add_rsqrt_fusion) | copy-start | bytes 1540
  65.3 210.5 %copy-start.22 = (pred[128,128]{0,1:T(8,128)(4,1)}, pred[128,128]{0,1:T(8,128)(4,1)S(1)}, u32[]{:S(2)}) copy-start(pred[128,128]{0,1:T(8,128)(4,1)S(1)} %fusion.56) | copy-start | bytes 49156
  275.0 90.8 %copy-start.12 = (bf16[128,8,192]{2,0,1:T(8,128)(2,1)}, bf16[128,8,192]{2,0,1:T(8,128)(2,1)S(1)}, u32[]{:S(2)}) copy-start(bf16[128,8,192]{2,0,1:T(8,128)(2,1)S(1)} %copy.146) | copy-start | bytes 1179652
  275.8 4.7 copy-start.13
  275.8 89.1 %copy-start.15 = (bf16[128,8,32]{2,0,1:T(8,128)(2,1)}, bf16[128,8,32]{2,0,1:T(8,128)(2,1)S(1)}, u32[]{:S(2)}) copy-start(bf16[128,8,32]{2,0,1:T(8,128)(2,1)S(1)} %get-tuple-element.60) | copy-start | bytes 196612
  275.8 4.7 copy-start.1
  280.6 5.8 copy-start.2
  286.4 1070.9 %reduce-scatter.5.cloned.1.call-start = ((), (), s32[]{:S(2)}) async-start(), calls=%async_computation.8 | async-start | bytes 28311552 | tf_op jit(solution)/shard_map/reduce_scatter | solution.py:190
  361.0 3.9 copy-start.17
  362.0 3.8 copy-start.14
  368.3 5.1 copy-start.19
  368.3 5.1 copy-start.21
  368.6 19.7 copy-start.3
  370.6 17.7 copy-start.4
  373.4 14.9 copy-start.11
  388.4 28.6 %copy-start.24 = (bf16[1024]{0:T(1024)(128)(2,1)S(1)}, bf16[1024]{0:T(1024)(128)(2,1)}, u32[]{:S(2)}) copy-start(bf16[1024]{0:T(1024)(128)(2,1)} %param.27) | copy-start | bytes 6148
  388.4 1298.7 %reduce-scatter.11.cloned.1.call-start = ((), (), s32[]{:S(2)}) async-start(), calls=%async_computation.11 | async-start | bytes 37748736 | tf_op jit(solution)/shard_map/reduce_scatter | solution.py:139
  719.8 1297.3 %reduce-scatter.9.cloned.1.call-start = ((), (), s32[]{:S(2)}) async-start(), calls=%async_computation.10 | async-start | bytes 37748736 | tf_op jit(solution)/shard_map/reduce_scatter | solution.py:160
  1043.4 1262.6 %all-reduce.12.cloned.1.call-start = ((), (), s32[]{:S(2)}) async-start(), calls=%async_computation.12 | async-start | bytes 25165824 | tf_op jit(solution)/shard_map/psum | solution.py:214
  2071.6 92.0 %copy-start.7 = (f32[128,2048]{1,0:T(8,128)S(1)}, f32[128,2048]{1,0:T(8,128)}, u32[]{:S(2)}) copy-start(f32[128,2048]{1,0:T(8,128)} %fusion.71) | copy-start | bytes 3145732
  2160.1 5.1 copy-start.9
  2160.7 160.5 %copy-start.26 = (f32[256]{0:T(256)}, f32[256]{0:T(256)S(1)}, u32[]{:S(2)}) copy-start(f32[256]{0:T(256)S(1)} %convert_element_type.207) | copy-start | bytes 3076
  2308.9 3.5 copy-start.6
  2312.4 4.4 copy-start.5
  (12 other events, 22.8 us)
Sparse Core Ops, SparseCore 0:
  9.7 252.8 all-gather.11
  264.2 90.5 all-gather.13
  356.4 327.1 all-gather.15
  685.0 326.3 all-gather.17
  1014.3 91.5 reduce-scatter.6
  1108.1 249.0 reduce-scatter.4
  1359.7 327.3 reduce-scatter.10
  1689.7 327.3 reduce-scatter.8
  2019.9 286.0 all-reduce.11
where the time goes:
time: 2340 us; the launch traced here: 2330 us
  waiting for transfers between devices  1900 us (81%)
  blocking collectives  204 us (9%)
  matrix products  169 us (7%)
  other arithmetic  28.5 us (1%)
    reduce_scatter x1, waiting for transfers between devices, local(): lax.psum_scatter(d_up_w.astype(jnp.bfloat16), 'shard', scatter_dimension=...  330 us
    reduce_scatter x1, waiting for transfers between devices, local(): lax.psum_scatter(d_down_w.astype(jnp.bfloat16), 'shard', scatter_dimensio...  330 us
    all_gather x1, waiting for transfers between devices, local(): lax.all_gather(down_weight, 'shard', axis=0, tiled=True)  291 us
    reduce_scatter x1, waiting for transfers between devices, local(): lax.psum_scatter(d_qkv_w.astype(jnp.bfloat16), 'shard', scatter_dimension...  251 us
    all_gather x1, waiting for transfers between devices, local(): lax.all_gather(up_weight, 'shard', axis=0, tiled=True)  245 us
    all_gather x1, waiting for transfers between devices, local(): lax.all_gather(qkv_weight, 'shard', axis=0, tiled=True)  197 us
    psum x1, waiting for transfers between devices, local(): lax.psum(s_qkv_w.astype(jnp.bfloat16), 'rep').astype(jnp.float32)  122 us
    all_gather x1, waiting for transfers between devices, local(): lax.all_gather(out_weight, 'shard', axis=0, tiled=True)  68 us
  transfers between devices with their start and end apart: 9, of which 9 were waited for; matrix products, arithmetic and copies ran while one was open for 8% of the time, Pallas kernels for 0%

commit v1 on v0

v1 whole, which is shorter than its diff:
```python
import math

import jax
import jax.numpy as jnp
from jax import lax
from jax.sharding import PartitionSpec as P

HEADS = 8
ROT = 64
EPS = 1e-05
f32 = jnp.float32
bf16 = jnp.bfloat16
BOTH = ("rep", "shard")
SIZES = (4, 2, 2, 2, 4)


def coords():
    for y in range(4):
        for h in range(2):
            for c in range(2):
                for l in range(2):
                    for x in range(4):
                        yield (y, h, c, l, x)


def linear(t):
    y, h, c, l, x = (v % m for v, m in zip(t, SIZES))
    return ((y * 2 + h) * 2 + c) * 8 + l * 4 + x


def move(value, y=0, h=0, c=0, l=0, x=0):
    step = (y, h, c, l, x)
    pairs = [(linear(t), linear(tuple(a + b for a, b in zip(t, step)))) for t in coords()]
    return lax.ppermute(value, BOTH, pairs)


def pick(value, index, axis):
    return lax.dynamic_index_in_dim(value, index, axis, keepdims=False)


def ring_gather(own, axis, cut):
    below = move(own, **{axis: 1})
    above = move(own, **{axis: -1})
    far_low = move(below[:cut], **{axis: 1})
    far_high = move(above[cut:], **{axis: -1})
    return [own, above, jnp.concatenate([far_low, far_high], 0), below]


def ring_reduce(pieces, axis, cut):
    own, above, far, below = pieces
    low = move(far[:cut].astype(bf16), **{axis: 1})
    high = move(far[cut:].astype(bf16), **{axis: -1})
    up = jnp.concatenate([above[:cut].astype(f32) + low.astype(f32), above[cut:].astype(f32)], 0)
    down = jnp.concatenate([below[:cut].astype(f32), below[cut:].astype(f32) + high.astype(f32)], 0)
    from_below = move(up.astype(bf16), **{axis: 1})
    from_above = move(down.astype(bf16), **{axis: -1})
    return own.astype(f32) + from_below.astype(f32) + from_above.astype(f32)


def group_gather(own, cut):
    other = move(own, l=1)
    return ring_gather(own, "x", cut) + ring_gather(other, "x", cut)


def group_reduce(pieces, cut):
    other = ring_reduce(pieces[4:], "x", cut)
    crossed = move(other.astype(bf16), l=1)
    return ring_reduce(pieces[:4], "x", cut) + crossed.astype(f32)


def place(pieces, start, count, axis):
    full = jnp.stack(pieces + pieces[:-1], axis)
    return lax.dynamic_slice_in_dim(full, (count - start) % count, count, axis)


def rotate(value, cosine, sine):
    half = ROT // 2
    first = value[..., :half]
    second = value[..., half:ROT]
    return jnp.concatenate(
        [first * cosine - second * sine, second * cosine + first * sine, value[..., ROT:]], -1
    )


def gelu_slope(hidden):
    normal_cdf = 0.5 * (1.0 + jax.scipy.special.erf(hidden / math.sqrt(2.0)))
    normal_pdf = jnp.exp(-0.5 * hidden * hidden) / math.sqrt(2.0 * math.pi)
    return normal_cdf + hidden * normal_pdf


def dot(a, b, ca=1, cb=0):
    return lax.dot_general(a, b, (((ca,), (cb,)), ((), ())), preferred_element_type=f32)


def normalize(value):
    xf = value.astype(f32)
    centre = xf - jnp.mean(xf, -1, keepdims=True)
    inverse = lax.rsqrt(jnp.mean(centre * centre, -1, keepdims=True) + EPS)
    return centre * inverse, inverse


def local(
    tokens,
    doc_lengths,
    cotangent,
    ln1_gain,
    ln1_bias,
    ln2_gain,
    ln2_bias,
    qkv_weight,
    qkv_bias,
    out_weight,
    out_bias,
    up_weight,
    up_bias,
    down_weight,
    down_bias,
):
    rows, width = tokens.shape
    head = width // HEADS
    scale = head ** (-0.5)
    group = 8
    rep = lax.axis_index("rep")
    shard = lax.axis_index("shard")
    y, h, c = rep // 4, (rep // 2) % 2, rep % 2
    l, x = shard // 4, shard % 4
    ff = up_bias.shape[0]

    part = lax.dynamic_slice_in_dim(qkv_weight, y * 64 + c * 32, 32, 0).reshape(32, 3, 8, head)
    part_up = lax.dynamic_slice_in_dim(up_weight, y * 64 + c * 32, 32, 0).reshape(32, 8, ff)
    part = jnp.concatenate(
        [part.transpose(2, 0, 1, 3).reshape(8, 32, 3 * head), part_up.transpose(1, 0, 2)], -1
    )
    cols = part.shape[-1]
    part = lax.all_to_all(part, "shard", 0, 0)
    ring = ring_gather(part, "y", 4)
    mine = place(ring, y, 4, 1)
    yours = move(mine, c=1)
    w_mixed = jnp.where(
        c == 0, jnp.stack([mine, yours], 2), jnp.stack([yours, mine], 2)
    ).reshape(width, cols)
    w_qkv = w_mixed[:, : 3 * head]
    w_up = w_mixed[:, 3 * head :]

    small = jnp.concatenate(
        [ln1_gain, ln1_bias, ln2_gain, ln2_bias, qkv_bias, doc_lengths[0].astype(bf16)]
    )
    small = jnp.pad(small[None], ((0, 7), (0, width - small.shape[0])))
    pieces = group_gather(jnp.concatenate([tokens, small], 0), 72)
    x_all = jnp.concatenate([p[:rows] for p in pieces], 0)
    infos = jnp.stack([p[rows] for p in pieces], 0)
    dy_all = jnp.concatenate(group_gather(cotangent, 64), 0)

    spots = jnp.arange(8)
    wanted = ((spots // 4) ^ l) * 4 + (spots % 4 - x) % 4
    chosen = (wanted[:, None] == spots[None, :]).astype(bf16)
    ordered = dot(chosen, infos)
    gains = ordered[:, :1024].reshape(8, 4, 256).transpose(1, 0, 2).reshape(4, width)
    g1, b1, g2, b2 = gains[0], gains[1], gains[2], gains[3]
    qkv_b = ordered[:, 1024:1792].reshape(3, 8, head)
    qkv_b = pick(qkv_b, shard, 1).reshape(3 * head)
    lengths = infos[:, 1792:1795].astype(jnp.int32)

    ends = jnp.cumsum(lengths, 1)
    starts = ends - lengths
    steps_t = jnp.arange(rows, dtype=jnp.int32)
    segment = jnp.sum((steps_t[None, :, None] >= ends[:, None, :]).astype(jnp.int32), -1)
    slots = jnp.arange(lengths.shape[1], dtype=jnp.int32)
    begin = jnp.sum(
        jnp.where(segment[:, :, None] == slots[None, None, :], starts[:, None, :], 0), -1
    )
    position = (steps_t[None, :] - begin).astype(f32)
    freq = 10000.0 ** (-2.0 * jnp.arange(ROT // 2, dtype=f32) / ROT)
    angle = position[:, :, None] * freq[None, None, :]
    cosine = jnp.cos(angle)
    sine = jnp.sin(angle)
    allowed = (segment[:, :, None] == segment[:, None, :]) & (
        steps_t[None, None, :] <= steps_t[None, :, None]
    )

    normed, _ = normalize(x_all)
    h1 = (normed * g1 + b1).astype(bf16)
    h2 = (normed * g2 + b2).astype(bf16)

    hidden = dot(h2, w_up) + up_bias.astype(f32)
    active = jax.nn.gelu(hidden, approximate=False).astype(bf16)
    qkv = (dot(h1, w_qkv) + qkv_b).reshape(group, rows, 3 * head)
    ql = rotate(qkv[..., :head], cosine, sine).astype(bf16)
    kl = rotate(qkv[..., head : 2 * head], cosine, sine).astype(bf16)
    vl = qkv[..., 2 * head :].astype(bf16)
    scores = jnp.einsum("bqd,bkd->bqk", ql, kl, preferred_element_type=f32) * scale
    masked = jnp.where(allowed, scores, -1e30)
    shifted = jnp.exp(masked - jnp.max(masked, -1, keepdims=True))
    probs = shifted / jnp.sum(shifted, -1, keepdims=True)
    probs_low = probs.astype(bf16)
    attended = (
        jnp.einsum("bqk,bkd->bqd", probs_low, vl, preferred_element_type=f32)
        .astype(bf16)
        .reshape(group * rows, head)
    )
    both_bias = (out_bias.astype(f32) + down_bias.astype(f32))[None, :]
    wide_bias = lax.dynamic_update_slice(jnp.zeros((1, width), f32), both_bias, (0, shard * 256))
    mix = dot(attended, out_weight) + dot(active, down_weight) + wide_bias
    mix = mix.astype(bf16).reshape(group, rows, width)
    mixed = group_reduce([mix[k] for k in range(group)], 64)
    mixed = (tokens.astype(f32) + mixed).astype(bf16)

    d_down_w = dot(active, dy_all, 0, 0)
    d_out_w = dot(attended, dy_all, 0, 0)
    d_active = dot(dy_all, down_weight, 1, 1)
    d_hidden = (d_active * gelu_slope(hidden)).astype(bf16)
    d_up_w = dot(h2, d_hidden, 0, 0)
    d_attended = dot(dy_all, out_weight, 1, 1).astype(bf16).reshape(group, rows, head)
    d_value = jnp.einsum("bqk,bqd->bkd", probs_low, d_attended, preferred_element_type=f32)
    d_probs = jnp.einsum("bqd,bkd->bqk", d_attended, vl, preferred_element_type=f32)
    centred = d_probs - jnp.sum(d_probs * probs, -1, keepdims=True)
    d_scores = (probs * centred).astype(bf16)
    d_query = jnp.einsum("bqk,bkd->bqd", d_scores, kl, preferred_element_type=f32) * scale
    d_key = jnp.einsum("bqk,bqd->bkd", d_scores, ql, preferred_element_type=f32) * scale
    d_query = rotate(d_query, cosine, -sine)
    d_key = rotate(d_key, cosine, -sine)
    d_qkv = (
        jnp.concatenate([d_query, d_key, d_value], -1).astype(bf16).reshape(group * rows, 3 * head)
    )
    d_qkv_w = dot(h1, d_qkv, 0, 0)
    d_h1 = dot(d_qkv, w_qkv, 1, 1)
    d_h2 = dot(d_hidden, w_up, 1, 1)
    sums = (d_h1 * g1 + d_h2 * g2).astype(bf16).reshape(group, rows, width)
    own_sum = group_reduce([sums[k] for k in range(group)], 64)
    own_normed, own_inverse = normalize(tokens)
    tokens_grad = cotangent.astype(f32) + own_inverse * (
        own_sum
        - jnp.mean(own_sum, -1, keepdims=True)
        - own_normed * jnp.mean(own_sum * own_normed, -1, keepdims=True)
    )

    dy_sum = jnp.sum(dy_all.astype(f32), 0)
    dy_own = lax.dynamic_slice_in_dim(dy_sum, shard * 256, 256)
    up_b = jnp.sum(d_hidden.astype(f32), 0)
    qkv_bg = jnp.sum(d_qkv.astype(f32), 0).reshape(3, 1, head)
    wide_qkv = lax.dynamic_update_slice(jnp.zeros((3, 8, head), f32), qkv_bg, (0, shard, 0))
    wide_up = lax.dynamic_update_slice(jnp.zeros((8 * ff,), f32), up_b, (shard * ff,))
    wide_dy = lax.dynamic_update_slice(jnp.zeros((width,), f32), dy_own, (shard * 256,))
    smalls = lax.psum(
        jnp.concatenate(
            [
                jnp.sum(d_h1 * normed, 0),
                jnp.sum(d_h1, 0),
                jnp.sum(d_h2 * normed, 0),
                jnp.sum(d_h2, 0),
                wide_dy,
                wide_qkv.reshape(-1),
                wide_up,
            ]
        ).reshape(-1, 256),
        BOTH,
    ).reshape(-1)

    def small_at(start, size):
        return lax.dynamic_slice_in_dim(smalls, start + shard * size, size)

    def sum_rep(grad, axis, first):
        away = pick(grad, 1 - c, axis + 2).astype(bf16)
        kept = pick(grad, c, axis + 2) + move(away, c=1).astype(f32)
        for name in first:
            if name == "y":
                parts = [pick(kept, (y + k) % 4, axis) for k in range(4)]
                kept = ring_reduce(parts, "y", parts[0].shape[0] // 2)
            else:
                at = axis if first == "yh" else axis + 1
                away = pick(kept, 1 - h, at).astype(bf16)
                kept = pick(kept, h, at) + move(away, h=1).astype(f32)
        return kept.astype(bf16)

    def gather_rep(chunk, first):
        got = chunk
        for name in reversed(first):
            if name == "y":
                got = place(ring_gather(got, "y", got.shape[0] // 2), y, 4, 0)
            else:
                other = move(got, h=1)
                got = jnp.where(h == 0, jnp.stack([got, other]), jnp.stack([other, got]))
        if first == "hy":
            got = got.swapaxes(0, 1)
        other = move(got, c=1)
        return jnp.where(c == 0, jnp.stack([got, other], 2), jnp.stack([other, got], 2))

    late = jnp.concatenate([d_down_w.reshape(4, 2, 2, -1, width), d_out_w.reshape(4, 2, 2, -1, width)], 3)
    late = late.transpose(3, 0, 1, 2, 4)
    late = gather_rep(sum_rep(late, 1, "hy"), "hy").astype(f32)
    down_rows = down_weight.shape[0] // 16
    down_grad = late[:, :, :, :down_rows].reshape(down_weight.shape)
    out_grad = late[:, :, :, down_rows:].reshape(out_weight.shape)

    wide = jnp.concatenate([d_qkv_w, d_up_w], 1).reshape(8, 4, 2, 2, 16, cols)
    wide = sum_rep(wide, 1, "yh")
    wide = lax.all_to_all(wide, "shard", 0, 0).transpose(1, 0, 2)
    wide = gather_rep(wide, "yh").astype(f32).reshape(256, 8, cols)
    qkv_grad = wide[:, :, : 3 * head].reshape(256, 8, 3, head).transpose(0, 2, 1, 3)
    qkv_grad = qkv_grad.reshape(256, 3 * width)
    up_grad = wide[:, :, 3 * head :].reshape(256, 8 * ff)

    dy_total = small_at(4 * width, 256)
    return (
        mixed,
        tokens_grad,
        small_at(0, 256),
        small_at(width, 256),
        small_at(2 * width, 256),
        small_at(3 * width, 256),
        qkv_grad,
        small_at(5 * width, 768),
        out_grad,
        dy_total,
        up_grad,
        small_at(8 * width, ff),
        down_grad,
        dy_total,
    )


def solution(mesh):
    rows = P(BOTH, None)
    vector, matrix = P("shard"), P("shard", None)
    return jax.shard_map(
        local,
        mesh=mesh,
        in_specs=(rows, rows, rows, vector, vector, vector, vector)
        + (matrix, vector, matrix, vector, matrix, vector, matrix, vector),
        out_specs=(rows, rows, vector, vector, vector, vector)
        + (matrix, vector, matrix, vector, matrix, vector, matrix, vector),
        check_vma=False,
    )
```

time: 2340 us -> 636 us (0.27)
  waiting for transfers between devices: 1900 us -> 104 us
  blocking collectives: 204 us -> 0 us
  local copies, waits for them, and re-layouts: 9.6 us -> 172 us
  starting transfers between devices: 0.82 us -> 137 us
  matrix products: 169 us -> 97.3 us
  other arithmetic: 28.5 us -> 96.6 us
    reduce_scatter x4 -> x0, waiting for transfers between devices: 974 us -> none  [the longest x1 330 us: local(): lax.psum_scatter(d_up_w.astype(jnp.bfloat16), 'shard', scatter_dimension=...]
    all_gather x4 -> x0, waiting for transfers between devices: 801 us -> none  [the longest x1 291 us: local(): lax.all_gather(down_weight, 'shard', axis=0, tiled=True)]
    all_gather x8 -> x0, blocking collectives: 130 us -> none  [the longest x1 24.3 us: local(): lax.all_gather(qkv_bias, 'shard', axis=0, tiled=True)]
    ppermute x0 -> x65, starting transfers between devices: none -> 126 us  [move(): return lax.ppermute(value, BOTH, pairs)]
    psum x1, waiting for transfers between devices: 122 us -> 0.01 us  [local(): lax.psum(jnp.concatenate([jnp.sum(d_h1 * normed, 0), jnp.sum(d_h1, 0), jn...]
    ppermute x0 -> x65, waiting for transfers between devices: none -> 97.8 us  [move(): return lax.ppermute(value, BOTH, pairs)]
    dot_general x17 -> x18, matrix products: 167 us -> 94.5 us  [the longest x13 84.2 us: dot(): lax.dot_general(a, b, (((ca,), (cb,)), ((), ())), preferred_element_type=...]
    unnamed x90 -> x213, local copies, waits for them, and re-layouts: 5.87 us -> 61.1 us
  transfers between devices with their start and end apart: 9 -> 68, of which waited for: 9 -> 21; matrix products, arithmetic and copies ran while one was open for 8% -> 29% of each run, Pallas kernels for 0% -> 0%
where the time goes in v1:
time: 636 us; the launch traced here: 624 us
  local copies, waits for them, and re-layouts  172 us (27%)
  starting transfers between devices  137 us (22%)
  waiting for transfers between devices  104 us (16%)
  matrix products  97.3 us (15%)
  other arithmetic  96.6 us (15%)
  between operations  16.2 us (3%)
    ppermute x65, starting transfers between devices, move(): return lax.ppermute(value, BOTH, pairs)  126 us
    ppermute x65, waiting for transfers between devices, move(): return lax.ppermute(value, BOTH, pairs)  97.8 us
    dot_general x13, matrix products, dot(): lax.dot_general(a, b, (((ca,), (cb,)), ((), ())), preferred_element_type=...  84.2 us
    unnamed x213, local copies, waits for them, and re-layouts  61.1 us
    convert_element_type x1, local copies, waits for them, and re-layouts, local(): wide = gather_rep(wide, 'yh').astype(f32).reshape(256, 8, cols)  21.7 us
    concatenate x1, local copies, waits for them, and re-layouts, local(): wide = jnp.concatenate([d_qkv_w, d_up_w], 1).reshape(8, 4, 2, 2, 16, cols)  14.3 us
  transfers between devices with their start and end apart: 68, of which 21 were waited for; matrix products, arithmetic and copies ran while one was open for 29% of the time, Pallas kernels for 0%

profile of v1, /device:TPU:1, one launch (start us, length us, event | category | flops | bytes accessed | tf_op | source)
XLA Modules:
  0.0 623.8 jit_solution(12102924908143515452)
XLA Ops:
  34.6 10.0 %collective-permute-done.24 = bf16[128,2048]{1,0:T(8,128)(2,1)} collective-permute-done((bf16[128,2048]{1,0:T(8,128)(2,1)}, bf16[128,2048]{1,0:T(8,128)(2,1)}, u32[]{:S(2)}, u32[]{:S(2)}) %collective-permute-start.24) | collective-permute-done | bytes 524320 | tf_op jit(solution)/shard_map/ppermute | solution.py:34
  106.5 5.2 collective-permute-done.12
  120.2 13.4 %collective-permute-start.13 = (bf16[8,4,32,1792]{3,2,1,0:T(8,128)(2,1)}, bf16[8,4,32,1792]{3,2,1,0:T(8,128)(2,1)}, u32[]{:S(2)}, u32[]{:S(2)}) collective-permute-start(bf16[8,4,32,1792]{3,2,1,0:T(8,128)(2,1)} %constant_dynamic-slice_fusion.3), channel_id=1, source_target_pairs={{0,8},{1,9},{2,10},{3,11},{4,12},{5,13},{6,14},{7,15},{8,0},{9,1},... | collective-permute-start | bytes 11010056 | tf_op jit(solution)/shard_map/ppermute | solution.py:34
  194.4 7.7 %fusion.44 = f32[1024,2048]{1,0:T(8,128)} fusion(bf16[1024,768]{1,0:T(8,128)(2,1)S(1)} %concatenate.149, bf16[2048,1792]{1,0:T(8,128)(2,1)} %bitcast.248), kind=kOutput, calls=%fused_computation.71 | convolution fusion | flops 3221225472 | bytes 13107200 | tf_op jit(solution)/shard_map/dot_general | solution.py:92
  202.5 6.1 fusion.146
  208.6 13.3 %fusion.23 = (bf16[1024,1024]{1,0:T(8,128)(2,1)S(1)}, f32[1024,1024]{1,0:T(8,128)S(1)}) fusion(f32[1024]{0:T(1024)S(1)} %copy-done.62, bf16[2048,1792]{1,0:T(8,128)(2,1)S(1)} %bitcast.251, bf16[1024,2048]{1,0:T(8,128)(2,1)S(1)} %copy-done.3, f32[2048]{0:T(1024)S(1)} %bitcast.286, f32[2048]{0:T(1024)S(1)} %bitcast.280, f32[1024]{0:T(1024)S(1)} %copy-done.64, ...), kind=kOutput, calls=%fused_computation.40 | convolution fusion | flops 4376756224 | bytes 14708736 | tf_op jit(solution)/shard_map/dot_general | solution.py:92
  221.9 9.1 %fusion.159 = f32[1024,2048]{1,0:T(8,128)} fusion(bf16[1024,1024]{1,0:T(8,128)(2,1)S(1)} %get-tuple-element.94, bf16[1024,2048]{1,0:T(8,128)(2,1)} %constant_dynamic-update-slice_fusion.1), kind=kOutput, calls=%fused_computation.326 | convolution fusion | flops 4294967296 | bytes 14680064 | tf_op jit(solution)/shard_map/dot_general | solution.py:92
  231.0 6.7 %fusion.158 = f32[1024,2048]{1,0:T(8,128)} fusion(bf16[1024,1024]{1,0:T(8,128)(2,1)S(1)} %get-tuple-element.94, bf16[1024,2048]{1,0:T(8,128)(2,1)S(1)} %copy-done.71), kind=kOutput, calls=%fused_computation.325 | convolution fusion | flops 4294967296 | bytes 14680064 | tf_op jit(solution)/shard_map/dot_general | solution.py:92
  237.7 7.6 %convert_reduce_fusion.2 = (f32[1024]{0:T(1024)S(1)}, bf16[1024,1024]{1,0:T(8,128)(2,1)S(1)}) fusion(f32[1024,1024]{1,0:T(8,128)S(1)} %get-tuple-element.95, f32[1024]{0:T(1024)S(1)} %copy-done.62, bf16[1024,2048]{1,0:T(8,128)(2,1)} %constant_dynamic-update-slice_fusion.1, bf16[1024,2048]{1,0:T(8,128)(2,1)S(1)} %copy-done.71), kind=kOutput, calls=%fused_computation.49 | convolution fusion | flops 4308597760 | bytes 14688256 | tf_op jit(solution)/shard_map/dot_general | solution.py:92
  245.3 7.6 %fusion.143 = f32[2048,1024]{0,1:T(8,128)} fusion(bf16[1024,1024]{1,0:T(8,128)(2,1)S(1)} %get-tuple-element.97, bf16[1024,2048]{1,0:T(8,128)(2,1)S(1)} %copy-done.3, f32[2048]{0:T(1024)S(1)} %bitcast.287, f32[2048]{0:T(1024)S(1)} %bitcast.281, f32[1024]{0:T(1024)S(1)} %copy-done.64, f32[1024]{0:T(1024)S(1)} %copy-done.50), kind=kOutput, calls=%fused_computation.314 | convolution fusion | flops 4307550208 | bytes 14704640 | tf_op jit(solution)/shard_map/dot_general | solution.py:92
  252.9 9.0 %fusion.149 = (f32[2048]{0:T(1024)S(1)}, f32[2048]{0:T(1024)S(1)}, bf16[1024,2048]{1,0:T(8,128)(2,1)S(1)}, f32[2048]{0:T(1024)S(1)}, f32[2048]{0:T(1024)S(1)}) fusion(f32[1024]{0:T(1024)S(1)} %copy-done.64, f32[1024]{0:T(1024)S(1)} %copy-done.50, bf16[1024,2048]{1,0:T(8,128)(2,1)S(1)} %copy-done.3, f32[2048]{0:T(1024)S(1)} %bitcast.282, ...), kind=kOutput, calls=%fused_computation.316 | convolution fusion | flops 4322222080 | bytes 23126016 | tf_op jit(solution)/shard_map/dot_general | solution.py:92
  272.0 10.6 %pad_maximum_fusion = f32[2048,1792]{0,1:T(8,128)} fusion(f32[2048,1024]{0,1:T(8,128)} %fusion.143, f32[2048,768]{0,1:T(8,128)} %fusion.146), kind=kLoop, calls=%fused_computation.1 | loop fusion | flops 3670016 | bytes 29360128 | tf_op jit(solution)/shard_map/concatenate | solution.py:295
  282.6 14.3 %copy.163 = f32[2048,1792]{1,0:T(8,128)} copy(f32[2048,1792]{0,1:T(8,128)} %pad_maximum_fusion) | data formatting | bytes 29360128 | tf_op jit(solution)/shard_map/concatenate | solution.py:295
  297.0 5.5 fusion.43
  307.4 5.1 add_convert_fusion.1
  332.2 5.9 fusion.19
  343.4 6.2 bitcast_add_fusion
  355.4 11.3 %collective-permute-done.54 = bf16[80,4,2048]{2,0,1:T(8,128)(2,1)} collective-permute-done((bf16[80,4,2048]{2,0,1:T(8,128)(2,1)S(1)}, bf16[80,4,2048]{2,0,1:T(8,128)(2,1)}, u32[]{:S(2)}, u32[]{:S(2)}) %collective-permute-start.54) | collective-permute-done | bytes 1310752 | tf_op jit(solution)/shard_map/ppermute | solution.py:34
  388.6 16.0 %collective-permute-done.59 = bf16[80,2048]{1,0:T(8,128)(2,1)S(1)} collective-permute-done((bf16[80,2048]{1,0:T(8,128)(2,1)S(1)}, bf16[80,2048]{1,0:T(8,128)(2,1)S(1)}, u32[]{:S(2)}, u32[]{:S(2)}) %collective-permute-start.59) | collective-permute-done | bytes 327712 | tf_op jit(solution)/shard_map/ppermute | solution.py:34
  420.7 6.6 %all-to-all-start.1 = ((bf16[8,16,1792]{2,1,0:T(8,128)(2,1)}), bf16[8,16,1792]{2,1,0:T(8,128)(2,1)S(1)}, u32[]{:S(2)}, u32[]{:S(2)}) async-start(bf16[8,16,1792]{2,1,0:T(8,128)(2,1)} %fusion.71), calls=%async_computation.1 | async-start | bytes 917504 | tf_op jit(solution)/shard_map/all_to_all | solution.py:297
  428.0 6.4 %all-to-all-done.1 = bf16[8,16,1792]{2,1,0:T(8,128)(2,1)S(1)} async-done(((bf16[8,16,1792]{2,1,0:T(8,128)(2,1)}), bf16[8,16,1792]{2,1,0:T(8,128)(2,1)S(1)}, u32[]{:S(2)}, u32[]{:S(2)}) %all-to-all-start.1) | async-done | bytes 458784 | tf_op jit(solution)/shard_map/all_to_all | solution.py:297
  437.2 6.1 collective-permute-done.47
  449.6 6.5 %collective-permute-done.48 = bf16[2,16,8,1792]{3,1,2,0:T(8,128)(2,1)S(1)} collective-permute-done((bf16[2,16,8,1792]{3,1,2,0:T(8,128)(2,1)S(1)}, bf16[2,16,8,1792]{3,1,2,0:T(8,128)(2,1)S(1)}, u32[]{:S(2)}, u32[]{:S(2)}) %collective-permute-start.48) | collective-permute-done | bytes 917536 | tf_op jit(solution)/shard_map/ppermute | solution.py:34
  459.5 6.9 %collective-permute-done.51 = bf16[1,16,8,1792]{3,1,2,0:T(8,128)(2,1)S(1)} collective-permute-done((bf16[1,16,8,1792]{3,1,2,0:T(8,128)(2,1)S(1)}, bf16[1,16,8,1792]{3,1,2,0:T(8,128)(2,1)S(1)}, u32[]{:S(2)}, u32[]{:S(2)}) %collective-permute-start.51) | collective-permute-done | bytes 458784 | tf_op jit(solution)/shard_map/ppermute | solution.py:34
  472.2 18.8 %collective-permute-start.52 = (bf16[4,2,16,8,1792]{4,2,3,1,0:T(8,128)(2,1)}, bf16[4,2,16,8,1792]{4,2,3,1,0:T(8,128)(2,1)}, u32[]{:S(2)}, u32[]{:S(2)}) collective-permute-start(bf16[4,2,16,8,1792]{4,2,3,1,0:T(8,128)(2,1)} %constant_dynamic-slice_fusion.1), channel_id=1, source_target_pairs={{0,8},{1,9},{2,10},{3,11},{4,12},{5,13},{6,14},{7,15},{8,0},{9,1},... | collective-permute-start | bytes 11010056 | tf_op jit(solution)/shard_map/ppermute | solution.py:34
  498.2 12.1 %collective-permute-start.64 = (bf16[4,2,80,2048]{3,2,0,1:T(8,128)(2,1)}, bf16[4,2,80,2048]{3,2,0,1:T(8,128)(2,1)}, u32[]{:S(2)}, u32[]{:S(2)}) collective-permute-start(bf16[4,2,80,2048]{3,2,0,1:T(8,128)(2,1)} %get-tuple-element.56), channel_id=1, source_target_pairs={{0,8},{1,9},{2,10},{3,11},{4,12},{5,13},{6,14},{7,15},{8,0},{9,1},... | collective-permute-start | bytes 7864328 | tf_op jit(solution)/shard_map/ppermute | solution.py:34
  517.8 9.1 %collective-permute-done.33 = bf16[128,2048]{1,0:T(8,128)(2,1)} collective-permute-done((bf16[128,2048]{1,0:T(8,128)(2,1)S(1)}, bf16[128,2048]{1,0:T(8,128)(2,1)}, u32[]{:S(2)}, u32[]{:S(2)}) %collective-permute-start.33) | collective-permute-done | bytes 524320 | tf_op jit(solution)/shard_map/ppermute | solution.py:34
  533.6 7.5 %collective-permute-done.15 = bf16[128,2048]{1,0:T(8,128)(2,1)} collective-permute-done((bf16[128,2048]{1,0:T(8,128)(2,1)}, bf16[128,2048]{1,0:T(8,128)(2,1)}, u32[]{:S(2)}, u32[]{:S(2)}) %collective-permute-start.15) | collective-permute-done | bytes 524320 | tf_op jit(solution)/shard_map/ppermute | solution.py:34
  560.7 9.9 %fusion.14 = f32[4,2,2,16,8,1792]{5,3,4,1,0,2:T(8,128)} fusion(bf16[4,2,1,16,8,1792]{5,3,4,1,0,2:T(8,128)(2,1)} %bitcast.51, bf16[4,2,1,16,8,1792]{5,3,4,1,0,2:T(8,128)(2,1)S(1)} %copy-done.8, pred[]{:T(512)S(6)} %eq.72), kind=kLoop, calls=%fused_computation.26 | loop fusion | flops 14680064 | bytes 22020096 | tf_op jit(solution)/shard_map/convert_element_type | solution.py:298
  570.6 21.7 %copy.167 = f32[4,2,2,16,8,1792]{5,4,3,2,1,0:T(8,128)} copy(f32[4,2,2,16,8,1792]{5,3,4,1,0,2:T(8,128)} %fusion.14) | data formatting | bytes 29360128 | tf_op jit(solution)/shard_map/convert_element_type | solution.py:298
  599.9 5.3 copy.203
  605.2 11.0 %copy.204 = f32[32,8,8,1024]{3,1,2,0:T(8,128)} copy(f32[32,8,8,1024]{3,2,1,0:T(8,128)S(1)} %bitcast.242) | data formatting | bytes 16777216
  (506 shorter events, 308.9 us)
Async XLA Ops:
  14.4 38.5 %collective-permute-start = (bf16[136,2048]{1,0:T(8,128)(2,1)}, bf16[136,2048]{1,0:T(8,128)(2,1)}, u32[]{:S(2)}, u32[]{:S(2)}) collective-permute-start(bf16[136,2048]{1,0:T(8,128)(2,1)} %pad_maximum_fusion.4), channel_id=1, source_target_pairs={{0,3},{1,0},{2,1},{3,2},{4,7},{5,4},{6,5},{7,6},{8,11},{9,8},{10,9... | collective-permute-start | bytes 1671176 | tf_op jit(solution)/shard_map/ppermute | solution.py:34
  17.8 38.9 %collective-permute-start.2 = (bf16[136,2048]{1,0:T(8,128)(2,1)}, bf16[136,2048]{1,0:T(8,128)(2,1)}, u32[]{:S(2)}, u32[]{:S(2)}) collective-permute-start(bf16[136,2048]{1,0:T(8,128)(2,1)} %pad_maximum_fusion.4), channel_id=1, source_target_pairs={{0,1},{1,2},{2,3},{3,0},{4,5},{5,6},{6,7},{7,4},{8,9},{9,10},{10,1... | collective-permute-start | bytes 1671176 | tf_op jit(solution)/shard_map/ppermute | solution.py:34
  17.8 29.5 %collective-permute-start.23 = (bf16[128,2048]{1,0:T(8,128)(2,1)}, bf16[128,2048]{1,0:T(8,128)(2,1)}, u32[]{:S(2)}, u32[]{:S(2)}) collective-permute-start(bf16[128,2048]{1,0:T(8,128)(2,1)} %param.17), channel_id=1, source_target_pairs={{0,3},{1,0},{2,1},{3,2},{4,7},{5,4},{6,5},{7,6},{8,11},{9,8},{10,9... | collective-permute-start | bytes 1572872 | tf_op jit(solution)/shard_map/ppermute | solution.py:34
  20.4 24.2 %collective-permute-start.24 = (bf16[128,2048]{1,0:T(8,128)(2,1)}, bf16[128,2048]{1,0:T(8,128)(2,1)}, u32[]{:S(2)}, u32[]{:S(2)}) collective-permute-start(bf16[128,2048]{1,0:T(8,128)(2,1)} %param.17), channel_id=1, source_target_pairs={{0,1},{1,2},{2,3},{3,0},{4,5},{5,6},{6,7},{7,4},{8,9},{9,10},{10,1... | collective-permute-start | bytes 1572872 | tf_op jit(solution)/shard_map/ppermute | solution.py:34
  20.4 29.8 %collective-permute-start.27 = (bf16[128,2048]{1,0:T(8,128)(2,1)}, bf16[128,2048]{1,0:T(8,128)(2,1)}, u32[]{:S(2)}, u32[]{:S(2)}) collective-permute-start(bf16[128,2048]{1,0:T(8,128)(2,1)} %param.17), channel_id=1, source_target_pairs={{0,4},{1,5},{2,6},{3,7},{4,0},{5,1},{6,2},{7,3},{8,12},{9,13},{10,... | collective-permute-start | bytes 1572872 | tf_op jit(solution)/shard_map/ppermute | solution.py:34
  24.8 47.9 %all-to-all-start = ((bf16[8,32,1792]{2,1,0:T(8,128)(2,1)}), bf16[8,32,1792]{2,1,0:T(8,128)(2,1)S(1)}, u32[]{:S(2)}, u32[]{:S(2)}) async-start(bf16[8,32,1792]{2,1,0:T(8,128)(2,1)} %copy.134), calls=%async_computation | async-start | bytes 1835008 | tf_op jit(solution)/shard_map/all_to_all | solution.py:135
  28.7 498.7 %all-reduce.3.cloned.1.call-start = ((), (), s32[]{:S(2)}) async-start(), calls=%async_computation.2 | async-start | bytes 196608 | tf_op jit(solution)/shard_map/psum | solution.py:244
  52.9 29.7 %collective-permute-start.28 = (bf16[128,2048]{1,0:T(8,128)(2,1)}, bf16[128,2048]{1,0:T(8,128)(2,1)}, u32[]{:S(2)}, u32[]{:S(2)}) collective-permute-start(bf16[128,2048]{1,0:T(8,128)(2,1)} %collective-permute-done.27), channel_id=1, source_target_pairs={{0,3},{1,0},{2,1},{3,2},{4,7},{5,4},{6,5},{7,6},{8,11},{9,8},{10,9... | collective-permute-start | bytes 1572872 | tf_op jit(solution)/shard_map/ppermute | solution.py:34
  56.7 25.9 %collective-permute-start.29 = (bf16[128,2048]{1,0:T(8,128)(2,1)}, bf16[128,2048]{1,0:T(8,128)(2,1)S(1)}, u32[]{:S(2)}, u32[]{:S(2)}) collective-permute-start(bf16[128,2048]{1,0:T(8,128)(2,1)} %collective-permute-done.27), channel_id=1, source_target_pairs={{0,1},{1,2},{2,3},{3,0},{4,5},{5,6},{6,7},{7,4},{8,9},{9,10},{10,1... | collective-permute-start | bytes 1572872 | tf_op jit(solution)/shard_map/ppermute | solution.py:34
  65.5 20.1 %collective-permute-start.4 = (bf16[136,2048]{1,0:T(8,128)(2,1)}, bf16[136,2048]{1,0:T(8,128)(2,1)}, u32[]{:S(2)}, u32[]{:S(2)}) collective-permute-start(bf16[136,2048]{1,0:T(8,128)(2,1)} %collective-permute-done.3), channel_id=1, source_target_pairs={{0,3},{1,0},{2,1},{3,2},{4,7},{5,4},{6,5},{7,6},{8,11},{9,8},{10,9... | collective-permute-start | bytes 1671176 | tf_op jit(solution)/shard_map/ppermute | solution.py:34
  74.3 29.2 %collective-permute-start.9 = (bf16[8,32,1792]{2,1,0:T(8,128)(2,1)S(1)}, bf16[8,32,1792]{2,1,0:T(8,128)(2,1)S(1)}, u32[]{:S(2)}, u32[]{:S(2)}) collective-permute-start(bf16[8,32,1792]{2,1,0:T(8,128)(2,1)S(1)} %all-to-all-done), channel_id=1, source_target_pairs={{0,96},{1,97},{2,98},{3,99},{4,100},{5,101},{6,102},{7,103},{8,104... | collective-permute-start | bytes 2752520 | tf_op jit(solution)/shard_map/ppermute | solution.py:34
  82.6 23.7 %collective-permute-start.10 = (bf16[8,32,1792]{2,1,0:T(8,128)(2,1)S(1)}, bf16[8,32,1792]{2,1,0:T(8,128)(2,1)S(1)}, u32[]{:S(2)}, u32[]{:S(2)}) collective-permute-start(bf16[8,32,1792]{2,1,0:T(8,128)(2,1)S(1)} %all-to-all-done), channel_id=1, source_target_pairs={{0,32},{1,33},{2,34},{3,35},{4,36},{5,37},{6,38},{7,39},{8,40},{9,... | collective-permute-start | bytes 2752520 | tf_op jit(solution)/shard_map/ppermute | solution.py:34
  92.0 41.8 %collective-permute-start.5 = (bf16[64,2048]{1,0:T(8,128)(2,1)S(1)}, bf16[64,2048]{1,0:T(8,128)(2,1)S(1)}, u32[]{:S(2)}, u32[]{:S(2)}) collective-permute-start(bf16[64,2048]{1,0:T(8,128)(2,1)S(1)} %slice.511), channel_id=1, source_target_pairs={{0,3},{1,0},{2,1},{3,2},{4,7},{5,4},{6,5},{7,6},{8,11},{9,8},{10,9... | collective-permute-start | bytes 786440 | tf_op jit(solution)/shard_map/ppermute | solution.py:34
  92.3 44.3 %collective-permute-start.8 = (bf16[72,2048]{1,0:T(8,128)(2,1)S(1)}, bf16[72,2048]{1,0:T(8,128)(2,1)}, u32[]{:S(2)}, u32[]{:S(2)}) collective-permute-start(bf16[72,2048]{1,0:T(8,128)(2,1)S(1)} %slice.520), channel_id=1, source_target_pairs={{0,1},{1,2},{2,3},{3,0},{4,5},{5,6},{6,7},{7,4},{8,9},{9,10},{10,1... | collective-permute-start | bytes 884744 | tf_op jit(solution)/shard_map/ppermute | solution.py:34
  120.2 26.2 %collective-permute-start.13 = (bf16[8,4,32,1792]{3,2,1,0:T(8,128)(2,1)}, bf16[8,4,32,1792]{3,2,1,0:T(8,128)(2,1)}, u32[]{:S(2)}, u32[]{:S(2)}) collective-permute-start(bf16[8,4,32,1792]{3,2,1,0:T(8,128)(2,1)} %constant_dynamic-slice_fusion.3), channel_id=1, source_target_pairs={{0,8},{1,9},{2,10},{3,11},{4,12},{5,13},{6,14},{7,15},{8,0},{9,1},... | collective-permute-start | bytes 11010056 | tf_op jit(solution)/shard_map/ppermute | solution.py:34
  265.1 49.7 %collective-permute-start.32 = (bf16[64,2048]{1,0:T(8,128)(2,1)}, bf16[64,2048]{1,0:T(8,128)(2,1)}, u32[]{:S(2)}, u32[]{:S(2)}) collective-permute-start(bf16[64,2048]{1,0:T(8,128)(2,1)} %get-tuple-element.31), channel_id=1, source_target_pairs={{0,1},{1,2},{2,3},{3,0},{4,5},{5,6},{6,7},{7,4},{8,9},{9,10},{10,1... | collective-permute-start | bytes 786440 | tf_op jit(solution)/shard_map/ppermute | solution.py:34
  265.1 50.8 %collective-permute-start.38 = (bf16[64,2048]{1,0:T(8,128)(2,1)}, bf16[64,2048]{1,0:T(8,128)(2,1)}, u32[]{:S(2)}, u32[]{:S(2)}) collective-permute-start(bf16[64,2048]{1,0:T(8,128)(2,1)} %get-tuple-element.32), channel_id=1, source_target_pairs={{0,3},{1,0},{2,1},{3,2},{4,7},{5,4},{6,5},{7,6},{8,11},{9,8},{10,9... | collective-permute-start | bytes 786440 | tf_op jit(solution)/shard_map/ppermute | solution.py:34
  268.2 47.8 %collective-permute-start.36 = (bf16[64,2048]{1,0:T(8,128)(2,1)}, bf16[64,2048]{1,0:T(8,128)(2,1)}, u32[]{:S(2)}, u32[]{:S(2)}) collective-permute-start(bf16[64,2048]{1,0:T(8,128)(2,1)} %get-tuple-element.35), channel_id=1, source_target_pairs={{0,1},{1,2},{2,3},{3,0},{4,5},{5,6},{6,7},{7,4},{8,9},{9,10},{10,1... | collective-permute-start | bytes 786440 | tf_op jit(solution)/shard_map/ppermute | solution.py:34
  268.2 50.4 %collective-permute-start.34 = (bf16[64,2048]{1,0:T(8,128)(2,1)}, bf16[64,2048]{1,0:T(8,128)(2,1)}, u32[]{:S(2)}, u32[]{:S(2)}) collective-permute-start(bf16[64,2048]{1,0:T(8,128)(2,1)} %get-tuple-element.36), channel_id=1, source_target_pairs={{0,3},{1,0},{2,1},{3,2},{4,7},{5,4},{6,5},{7,6},{8,11},{9,8},{10,9... | collective-permute-start | bytes 786440 | tf_op jit(solution)/shard_map/ppermute | solution.py:34
  302.4 40.9 %collective-permute-start.41 = (bf16[8,4,2,16,1792]{4,3,2,1,0:T(8,128)(2,1)}, bf16[8,4,2,16,1792]{4,3,2,1,0:T(8,128)(2,1)}, u32[]{:S(2)}, u32[]{:S(2)}) collective-permute-start(bf16[8,4,2,16,1792]{4,3,2,1,0:T(8,128)(2,1)} %fusion.43), channel_id=1, source_target_pairs={{0,8},{1,9},{2,10},{3,11},{4,12},{5,13},{6,14},{7,15},{8,0},{9,1},... | collective-permute-start | bytes 11010056 | tf_op jit(solution)/shard_map/ppermute | solution.py:34
  326.5 171.6 %collective-permute-start.39 = (bf16[128,2048]{1,0:T(8,128)(2,1)}, bf16[128,2048]{1,0:T(8,128)(2,1)}, u32[]{:S(2)}, u32[]{:S(2)}) collective-permute-start(bf16[128,2048]{1,0:T(8,128)(2,1)} %pad_maximum_fusion.16), channel_id=1, source_target_pairs={{0,3},{1,0},{2,1},{3,2},{4,7},{5,4},{6,5},{7,6},{8,11},{9,8},{10,9... | collective-permute-start | bytes 1572872 | tf_op jit(solution)/shard_map/ppermute | solution.py:34
  340.0 26.7 %collective-permute-start.54 = (bf16[80,4,2048]{2,0,1:T(8,128)(2,1)S(1)}, bf16[80,4,2048]{2,0,1:T(8,128)(2,1)}, u32[]{:S(2)}, u32[]{:S(2)}) collective-permute-start(bf16[80,4,2048]{2,0,1:T(8,128)(2,1)S(1)} %fusion.53), channel_id=1, source_target_pairs={{0,16},{1,17},{2,18},{3,19},{4,20},{5,21},{6,22},{7,23},{8,24},{9,... | collective-permute-start | bytes 3932168 | tf_op jit(solution)/shard_map/ppermute | solution.py:34
  352.0 24.9 %collective-permute-start.44 = (bf16[4,2,16,1792]{3,2,1,0:T(8,128)(2,1)S(1)}, bf16[4,2,16,1792]{3,2,1,0:T(8,128)(2,1)S(1)}, u32[]{:S(2)}, u32[]{:S(2)}) collective-permute-start(bf16[4,2,16,1792]{3,2,1,0:T(8,128)(2,1)S(1)} %get-tuple-element.68), channel_id=1, source_target_pairs={{0,96},{1,97},{2,98},{3,99},{4,100},{5,101},{6,102},{7,103},{8,104... | collective-permute-start | bytes 1376264 | tf_op jit(solution)/shard_map/ppermute | solution.py:34
  352.1 29.0 %collective-permute-start.42 = (bf16[4,2,16,1792]{3,2,1,0:T(8,128)(2,1)S(1)}, bf16[4,2,16,1792]{3,2,1,0:T(8,128)(2,1)S(1)}, u32[]{:S(2)}, u32[]{:S(2)}) collective-permute-start(bf16[4,2,16,1792]{3,2,1,0:T(8,128)(2,1)S(1)} %get-tuple-element.67), channel_id=1, source_target_pairs={{0,32},{1,33},{2,34},{3,35},{4,36},{5,37},{6,38},{7,39},{8,40},{9,... | collective-permute-start | bytes 1376264 | tf_op jit(solution)/shard_map/ppermute | solution.py:34
  378.3 30.6 %collective-permute-start.45 = (bf16[8,2,16,1792]{3,2,1,0:T(8,128)(2,1)S(1)}, bf16[8,2,16,1792]{3,2,1,0:T(8,128)(2,1)S(1)}, u32[]{:S(2)}, u32[]{:S(2)}) collective-permute-start(bf16[8,2,16,1792]{3,2,1,0:T(8,128)(2,1)S(1)} %pad_maximum_fusion.3), channel_id=1, source_target_pairs={{0,96},{1,97},{2,98},{3,99},{4,100},{5,101},{6,102},{7,103},{8,104... | collective-permute-start | bytes 2752520 | tf_op jit(solution)/shard_map/ppermute | solution.py:34
  381.2 27.8 %collective-permute-start.43 = (bf16[8,2,16,1792]{3,2,1,0:T(8,128)(2,1)S(1)}, bf16[8,2,16,1792]{3,2,1,0:T(8,128)(2,1)S(1)}, u32[]{:S(2)}, u32[]{:S(2)}) collective-permute-start(bf16[8,2,16,1792]{3,2,1,0:T(8,128)(2,1)S(1)} %pad_maximum_fusion.2), channel_id=1, source_target_pairs={{0,32},{1,33},{2,34},{3,35},{4,36},{5,37},{6,38},{7,39},{8,40},{9,... | collective-permute-start | bytes 2752520 | tf_op jit(solution)/shard_map/ppermute | solution.py:34
  404.6 93.6 %collective-permute-start.37 = (bf16[128,2048]{1,0:T(8,128)(2,1)}, bf16[128,2048]{1,0:T(8,128)(2,1)}, u32[]{:S(2)}, u32[]{:S(2)}) collective-permute-start(bf16[128,2048]{1,0:T(8,128)(2,1)} %pad_maximum_fusion.15), channel_id=1, source_target_pairs={{0,1},{1,2},{2,3},{3,0},{4,5},{5,6},{6,7},{7,4},{8,9},{9,10},{10,1... | collective-permute-start | bytes 1572872 | tf_op jit(solution)/shard_map/ppermute | solution.py:34
  414.3 97.6 %collective-permute-start.21 = (bf16[128,2048]{1,0:T(8,128)(2,1)}, bf16[128,2048]{1,0:T(8,128)(2,1)}, u32[]{:S(2)}, u32[]{:S(2)}) collective-permute-start(bf16[128,2048]{1,0:T(8,128)(2,1)} %pad_maximum_fusion.12), channel_id=1, source_target_pairs={{0,3},{1,0},{2,1},{3,2},{4,7},{5,4},{6,5},{7,6},{8,11},{9,8},{10,9... | collective-permute-start | bytes 1572872 | tf_op jit(solution)/shard_map/ppermute | solution.py:34
  466.3 26.2 %collective-permute-start.63 = (bf16[4,80,2048]{2,1,0:T(8,128)(2,1)S(1)}, bf16[4,80,2048]{2,1,0:T(8,128)(2,1)S(1)}, u32[]{:S(2)}, u32[]{:S(2)}) collective-permute-start(bf16[4,80,2048]{2,1,0:T(8,128)(2,1)S(1)} %constant_dynamic-slice_fusion), channel_id=1, source_target_pairs={{0,16},{1,17},{2,18},{3,19},{4,20},{5,21},{6,22},{7,23},{8,24},{9,... | collective-permute-start | bytes 3932168 | tf_op jit(solution)/shard_map/ppermute | solution.py:34
  472.2 88.4 %collective-permute-start.52 = (bf16[4,2,16,8,1792]{4,2,3,1,0:T(8,128)(2,1)}, bf16[4,2,16,8,1792]{4,2,3,1,0:T(8,128)(2,1)}, u32[]{:S(2)}, u32[]{:S(2)}) collective-permute-start(bf16[4,2,16,8,1792]{4,2,3,1,0:T(8,128)(2,1)} %constant_dynamic-slice_fusion.1), channel_id=1, source_target_pairs={{0,8},{1,9},{2,10},{3,11},{4,12},{5,13},{6,14},{7,15},{8,0},{9,1},... | collective-permute-start | bytes 11010056 | tf_op jit(solution)/shard_map/ppermute | solution.py:34
  492.5 20.9 %collective-permute-start.19 = (bf16[128,2048]{1,0:T(8,128)(2,1)S(1)}, bf16[128,2048]{1,0:T(8,128)(2,1)S(1)}, u32[]{:S(2)}, u32[]{:S(2)}) collective-permute-start(bf16[128,2048]{1,0:T(8,128)(2,1)S(1)} %copy-done.43), channel_id=1, source_target_pairs={{0,1},{1,2},{2,3},{3,0},{4,5},{5,6},{6,7},{7,4},{8,9},{9,10},{10,1... | collective-permute-start | bytes 1572872 | tf_op jit(solution)/shard_map/ppermute | solution.py:34
  498.2 51.6 %collective-permute-start.64 = (bf16[4,2,80,2048]{3,2,0,1:T(8,128)(2,1)}, bf16[4,2,80,2048]{3,2,0,1:T(8,128)(2,1)}, u32[]{:S(2)}, u32[]{:S(2)}) collective-permute-start(bf16[4,2,80,2048]{3,2,0,1:T(8,128)(2,1)} %get-tuple-element.56), channel_id=1, source_target_pairs={{0,8},{1,9},{2,10},{3,11},{4,12},{5,13},{6,14},{7,15},{8,0},{9,1},... | collective-permute-start | bytes 7864328 | tf_op jit(solution)/shard_map/ppermute | solution.py:34
  (116 other events, 1355.5 us)
Sparse Core Ops, SparseCore 0:
  272.1 138.7 all-reduce.2
